TPU v7x, 32 devices: a whole 2x2x4 slice. The times are simulated.
32 devices in a mesh: dp: 16 (over z, y, x), mp: 2 (over core).
Axes of the slice: x: 2, y: 2, z: 4, core: 2. Of those that a mesh axis runs over, the one named last changes fastest.
Arguments:
- tokens: bfloat16 [2, 96, 160, 768], P(None, ('dp', 'mp')), may hold values from -6 to 6
- lengths: int32 [2, 96], P(None, ('dp', 'mp')), may hold values from 95 to 160, as said below
- cotangent: bfloat16 [2, 96, 160, 768], P(None, ('dp', 'mp')), may hold values from -6 to 6
- attn_in: float32 [768, 3, 768], P('dp', None, 'mp')
- attn_out: float32 [768, 768], P('mp', 'dp')
- ffn_in: float32 [768, 3072], P('dp', 'mp')
- ffn_out: float32 [3072, 768], P('mp', 'dp')
- attn_in_first: float32 [768, 3, 768], P('dp', None, 'mp'), may hold values from -32 to 32
- attn_in_second: float32 [768, 3, 768], P('dp', None, 'mp'), may hold values from 2.7648 to 11.0592
- attn_out_first: float32 [768, 768], P('mp', 'dp'), may hold values from -56 to 56
- attn_out_second: float32 [768, 768], P('mp', 'dp'), may hold values from 7.68 to 30.72
- ffn_in_first: float32 [768, 3072], P('dp', 'mp'), may hold values from -56 to 56
- ffn_in_second: float32 [768, 3072], P('dp', 'mp'), may hold values from 7.68 to 30.72
- ffn_out_first: float32 [3072, 768], P('mp', 'dp'), may hold values from -64 to 64
- ffn_out_second: float32 [3072, 768], P('mp', 'dp'), may hold values from 11.0592 to 44.2368
- small: float32 [12, 768], replicated
- small_first: float32 [12, 768], replicated, may hold values from -56 to 56
- small_second: float32 [12, 768], replicated, may hold values from 7.68 to 30.72
Outputs:
- output: bfloat16 [2, 96, 160, 768], P(None, ('dp', 'mp'))
- tokens_grad: float32 [2, 96, 160, 768], P(None, ('dp', 'mp'))
- attn_in_grad: float32 [768, 3, 768], P('dp', None, 'mp')
- attn_in_first_new: float32 [768, 3, 768], P('dp', None, 'mp')
- attn_in_second_new: float32 [768, 3, 768], P('dp', None, 'mp')
- attn_in_new: float32 [768, 3, 768], P('dp', None, 'mp')
- attn_in_low: bfloat16 [768, 3, 768], P('dp', None, 'mp')
- attn_out_grad: float32 [768, 768], P('mp', 'dp')
- attn_out_first_new: float32 [768, 768], P('mp', 'dp')
- attn_out_second_new: float32 [768, 768], P('mp', 'dp')
- attn_out_new: float32 [768, 768], P('mp', 'dp')
- attn_out_low: bfloat16 [768, 768], P('mp', 'dp')
- ffn_in_grad: float32 [768, 3072], P('dp', 'mp')
- ffn_in_first_new: float32 [768, 3072], P('dp', 'mp')
- ffn_in_second_new: float32 [768, 3072], P('dp', 'mp')
- ffn_in_new: float32 [768, 3072], P('dp', 'mp')
- ffn_in_low: bfloat16 [768, 3072], P('dp', 'mp')
- ffn_out_grad: float32 [3072, 768], P('mp', 'dp')
- ffn_out_first_new: float32 [3072, 768], P('mp', 'dp')
- ffn_out_second_new: float32 [3072, 768], P('mp', 'dp')
- ffn_out_new: float32 [3072, 768], P('mp', 'dp')
- ffn_out_low: bfloat16 [3072, 768], P('mp', 'dp')
- small_grad: float32 [12, 768], replicated
- small_first_new: float32 [12, 768], replicated
- small_second_new: float32 [12, 768], replicated
- small_new: float32 [12, 768], replicated
- norms: float32 [2, 4], replicated
Inputs may be any that keep to these rules, and one draw needn't show every extreme that they name: `lengths`: true length of each chain; positions at or beyond it are padding; both ends of the range occur in every draw.
All inputs are finite; a program needn't handle non-finite values.
Results may differ from a plain program's by a relative error of at most 0.015.
The roundings to bfloat16 on the way count: a program that leaves them out, or rounds other values in their place, can miss the bound.
Values may be sent and summed in bfloat16 or wider, within the bound.
A program may use at most 192 MiB of HBM per device.

v0:
```python
import jax
import jax.numpy as jnp
from jax import lax
from jax.sharding import PartitionSpec as P

HEAD = 64
STEP = 10


NORM_EPS = 1e-05
RATE_MATRIX = 0.3
RATE_VECTOR = 0.2
BETA_FIRST = 0.9
BETA_SECOND = 0.999
ADAM_EPS = 1e-06
DECAY_RATE = 0.01
MASKED_SCORE = -1000000000.0


def normalize(hidden, gain, shift):
    center = hidden - jnp.mean(hidden, axis=-1, keepdims=True)
    spread = jnp.mean(center * center, axis=-1, keepdims=True)
    inverse = lax.rsqrt(spread + NORM_EPS)
    normed = center * inverse
    return (normed * gain + shift, normed, inverse)


def norm_back(upstream, normed, inverse, gain):
    scaled = upstream * gain
    centred = (
        scaled
        - jnp.mean(scaled, axis=-1, keepdims=True)
        - normed * jnp.mean(scaled * normed, axis=-1, keepdims=True)
    )
    return (
        centred * inverse,
        jnp.sum(upstream * normed, axis=(0, 1)),
        jnp.sum(upstream, axis=(0, 1)),
    )


def gelu_exact(values):
    return jax.nn.gelu(values, approximate=False)


def contract_rows(left, right):
    return lax.dot_general(
        left, right, (((0,), (0,)), ((), ())), preferred_element_type=jnp.float32
    )


def times_transposed(left, right):
    return lax.dot_general(
        left, right, (((1,), (1,)), ((), ())), preferred_element_type=jnp.float32
    )


def score_block(queries, key_rows, token_mask, score_scale):
    scores = (
        jnp.einsum("clhe,cshe->chls", queries, key_rows, preferred_element_type=jnp.float32)
        * score_scale
    )
    return jnp.where(token_mask[:, None, None, :], scores, MASKED_SCORE)


def placed(vector, length, start):
    return lax.dynamic_update_slice_in_dim(jnp.zeros((length,), jnp.float32), vector, start, 0)


def reduce_weights(local_grads):
    return (
        lax.psum_scatter(local_grads[0], "dp", scatter_dimension=0, tiled=True),
        lax.psum_scatter(local_grads[1], "dp", scatter_dimension=0, tiled=True),
        lax.psum_scatter(local_grads[2], "dp", scatter_dimension=1, tiled=True),
        lax.psum_scatter(local_grads[3], "dp", scatter_dimension=1, tiled=True),
    )


def adam_moments(gradient, first_moment, second_moment):
    first_new = BETA_FIRST * first_moment + (1.0 - BETA_FIRST) * gradient
    second_new = BETA_SECOND * second_moment + (1.0 - BETA_SECOND) * gradient * gradient
    direction = (
        first_new
        / (1.0 - BETA_FIRST**STEP)
        / (jnp.sqrt(second_new / (1.0 - BETA_SECOND**STEP)) + ADAM_EPS)
    )
    return (first_new, second_new, direction)


def body(
    tokens,
    lengths,
    cotangent,
    attn_in,
    attn_out,
    ffn_in,
    ffn_out,
    attn_in_first,
    attn_in_second,
    attn_out_first,
    attn_out_second,
    ffn_in_first,
    ffn_in_second,
    ffn_out_first,
    ffn_out_second,
    small,
    small_first,
    small_second,
):
    mp_index = lax.axis_index("mp")
    half_wide = attn_in.shape[2]
    half_inner = ffn_in.shape[1]
    width = small.shape[1]
    heads_here = half_wide // HEAD
    score_scale = HEAD ** (-0.5)
    w_in, w_up, w_mid, w_down = (
        lax.all_gather(attn_in.astype(jnp.bfloat16), "dp", axis=0, tiled=True),
        lax.all_gather(ffn_in.astype(jnp.bfloat16), "dp", axis=0, tiled=True),
        lax.all_gather(attn_out.astype(jnp.bfloat16), "dp", axis=1, tiled=True),
        lax.all_gather(ffn_out.astype(jnp.bfloat16), "dp", axis=1, tiled=True),
    )
    w_in_flat = w_in.reshape(width, 3 * half_wide)
    bias_query = lax.dynamic_slice_in_dim(small[0], mp_index * half_wide, half_wide)
    bias_value = lax.dynamic_slice_in_dim(small[1], mp_index * half_wide, half_wide)
    bias_upper = lax.dynamic_slice_in_dim(small[8:].reshape(-1), mp_index * half_inner, half_inner)
    out_blocks = []
    grad_blocks = []
    vector_total = jnp.zeros(small.shape, jnp.float32)
    weight_total = None
    for micro_index in range(tokens.shape[0]):
        own_tokens = tokens[micro_index]
        positions = own_tokens.shape[1]
        gathered, length_all = (
            lax.all_gather(own_tokens, "mp", axis=0, tiled=True),
            lax.all_gather(lengths[micro_index].astype(jnp.bfloat16), "mp", axis=0, tiled=True),
        )
        chain_count = gathered.shape[0]
        row_count = chain_count * positions
        token_mask = (
            jnp.arange(positions, dtype=jnp.float32)[None, :]
            < length_all.astype(jnp.float32)[:, None]
        )
        rows_in = gathered.reshape(row_count, width)
        packed = jnp.dot(rows_in, w_in_flat, preferred_element_type=jnp.float32).reshape(
            row_count, 3, half_wide
        )
        head_shape = (chain_count, positions, heads_here, HEAD)
        queries = (packed[:, 0] + bias_query).astype(jnp.bfloat16).reshape(head_shape)
        key_rows = packed[:, 1].astype(jnp.bfloat16).reshape(head_shape)
        value_rows = (packed[:, 2] + bias_value).astype(jnp.bfloat16).reshape(head_shape)
        scores = score_block(queries, key_rows, token_mask, score_scale)
        row_peak = jnp.max(scores, axis=-1, keepdims=True)
        exponent = jnp.exp(scores - row_peak)
        row_total = jnp.sum(exponent, axis=-1, keepdims=True)
        attention = exponent / row_total
        log_total = row_peak + jnp.log(row_total)
        context = (
            jnp.einsum(
                "chls,cshe->clhe",
                attention.astype(jnp.bfloat16),
                value_rows,
                preferred_element_type=jnp.float32,
            )
            .astype(jnp.bfloat16)
            .reshape(row_count, half_wide)
        )
        attn_terms = jnp.dot(context, w_mid, preferred_element_type=jnp.float32).reshape(
            chain_count, positions, width
        )
        attn_branch = lax.psum_scatter(attn_terms, "mp", scatter_dimension=0, tiled=True) + small[2]
        first_out, first_normed, first_inverse = normalize(
            own_tokens.astype(jnp.float32) + attn_branch, small[3], small[4]
        )
        ffn_rows = lax.all_gather(first_out.astype(jnp.bfloat16), "mp", axis=0, tiled=True).reshape(
            row_count, width
        )
        upper = jnp.dot(ffn_rows, w_up, preferred_element_type=jnp.float32) + bias_upper
        hidden_full, gelu_pull = jax.vjp(gelu_exact, upper)
        hidden = hidden_full.astype(jnp.bfloat16)
        down_terms = jnp.dot(hidden, w_down, preferred_element_type=jnp.float32).reshape(
            chain_count, positions, width
        )
        down_out = lax.psum_scatter(down_terms, "mp", scatter_dimension=0, tiled=True) + small[5]
        output, second_normed, second_inverse = normalize(first_out + down_out, small[6], small[7])
        out_blocks.append(output.astype(jnp.bfloat16))
        upstream = cotangent[micro_index].astype(jnp.float32)
        d_second, gain_two_grad, shift_two_grad = norm_back(
            upstream, second_normed, second_inverse, small[6]
        )
        d_down = d_second.astype(jnp.bfloat16)
        d_down_rows = lax.all_gather(d_down, "mp", axis=0, tiled=True).reshape(row_count, width)
        g_down = contract_rows(hidden, d_down_rows)
        d_hidden = times_transposed(d_down_rows, w_down)
        d_upper = gelu_pull(d_hidden)[0].astype(jnp.bfloat16)
        g_up = contract_rows(ffn_rows, d_upper)
        d_first_terms = times_transposed(d_upper, w_up).reshape(chain_count, positions, width)
        d_first = lax.psum_scatter(d_first_terms, "mp", scatter_dimension=0, tiled=True) + d_second
        d_attn_full, gain_one_grad, shift_one_grad = norm_back(
            d_first, first_normed, first_inverse, small[3]
        )
        d_attn = d_attn_full.astype(jnp.bfloat16)
        d_attn_rows = lax.all_gather(d_attn, "mp", axis=0, tiled=True).reshape(row_count, width)
        g_mid = contract_rows(context, d_attn_rows)
        d_context = times_transposed(d_attn_rows, w_mid).astype(jnp.bfloat16).reshape(head_shape)
        scores_again = score_block(queries, key_rows, token_mask, score_scale)
        attention_again = jnp.exp(scores_again - log_total)
        d_attention = jnp.einsum(
            "clhe,cshe->chls", d_context, value_rows, preferred_element_type=jnp.float32
        )
        d_scores = (
            attention_again
            * (d_attention - jnp.sum(attention_again * d_attention, axis=-1, keepdims=True))
        ).astype(jnp.bfloat16)
        d_queries = (
            (
                jnp.einsum(
                    "chls,cshe->clhe", d_scores, key_rows, preferred_element_type=jnp.float32
                )
                * score_scale
            )
            .astype(jnp.bfloat16)
            .reshape(row_count, half_wide)
        )
        d_keys = (
            (
                jnp.einsum("chls,clhe->cshe", d_scores, queries, preferred_element_type=jnp.float32)
                * score_scale
            )
            .astype(jnp.bfloat16)
            .reshape(row_count, half_wide)
        )
        d_values = (
            jnp.einsum(
                "chls,clhe->cshe",
                attention_again.astype(jnp.bfloat16),
                d_context,
                preferred_element_type=jnp.float32,
            )
            .astype(jnp.bfloat16)
            .reshape(row_count, half_wide)
        )
        d_packed = jnp.stack((d_queries, d_keys, d_values), axis=1).reshape(
            row_count, 3 * half_wide
        )
        g_in = contract_rows(rows_in, d_packed).reshape(width, 3, half_wide)
        d_in_terms = times_transposed(d_packed, w_in_flat).reshape(chain_count, positions, width)
        d_tokens = (
            lax.psum_scatter(
                d_in_terms.astype(jnp.bfloat16), "mp", scatter_dimension=0, tiled=True
            ).astype(jnp.float32)
            + d_attn_full
        )
        grad_blocks.append(d_tokens)
        head_rows = jnp.stack(
            (
                placed(jnp.sum(d_queries, axis=0, dtype=jnp.float32), width, mp_index * half_wide),
                placed(jnp.sum(d_values, axis=0, dtype=jnp.float32), width, mp_index * half_wide),
                jnp.sum(d_attn, axis=(0, 1), dtype=jnp.float32),
                gain_one_grad,
                shift_one_grad,
                jnp.sum(d_down, axis=(0, 1), dtype=jnp.float32),
                gain_two_grad,
                shift_two_grad,
            )
        )
        upper_rows = placed(
            jnp.sum(d_upper, axis=0, dtype=jnp.float32),
            (small.shape[0] - 8) * width,
            mp_index * half_inner,
        ).reshape(-1, width)
        vector_total = vector_total + jnp.concatenate((head_rows, upper_rows), axis=0)
        local_grads = (g_in, g_up, g_mid, g_down)
        weight_total = (
            local_grads
            if weight_total is None
            else jax.tree.map(jnp.add, weight_total, local_grads)
        )
    reduced = reduce_weights(weight_total)
    grad_in, grad_up, grad_mid, grad_down = reduced
    matrices = (
        (attn_in, grad_in, attn_in_first, attn_in_second),
        (attn_out, grad_mid, attn_out_first, attn_out_second),
        (ffn_in, grad_up, ffn_in_first, ffn_in_second),
        (ffn_out, grad_down, ffn_out_first, ffn_out_second),
    )
    moments = [adam_moments(entry[1], entry[2], entry[3]) for entry in matrices]
    headings = [
        moments[matrix_index][2] + DECAY_RATE * matrices[matrix_index][0]
        for matrix_index in range(4)
    ]
    weight_squares = jnp.stack([jnp.sum(entry[0] * entry[0]) for entry in matrices])
    step_squares = jnp.stack([jnp.sum(heading * heading) for heading in headings])
    vector_grad = lax.psum(vector_total, ("dp", "mp"))
    weight_sums, step_sums = lax.psum((weight_squares, step_squares), ("dp", "mp"))
    weight_norms = jnp.sqrt(weight_sums)
    step_norms = jnp.sqrt(step_sums)
    results = [jnp.stack(out_blocks), jnp.stack(grad_blocks)]
    for matrix_index in range(4):
        weight = matrices[matrix_index][0]
        renewed = (
            weight
            - RATE_MATRIX
            * (weight_norms[matrix_index] / step_norms[matrix_index])
            * headings[matrix_index]
        )
        results.extend(
            [
                matrices[matrix_index][1],
                moments[matrix_index][0],
                moments[matrix_index][1],
                renewed,
                renewed.astype(jnp.bfloat16),
            ]
        )
    small_first_new, small_second_new, small_direction = adam_moments(
        vector_grad, small_first, small_second
    )
    small_new = small - RATE_VECTOR * small_direction
    results.extend(
        [
            vector_grad,
            small_first_new,
            small_second_new,
            small_new,
            jnp.stack((weight_norms, step_norms)),
        ]
    )
    return tuple(results)


def solution(mesh):
    return jax.shard_map(
        body,
        mesh=mesh,
        in_specs=(
            P(None, ("dp", "mp"), None, None),
            P(None, ("dp", "mp")),
            P(None, ("dp", "mp"), None, None),
            P("dp", None, "mp"),
            P("mp", "dp"),
            P("dp", "mp"),
            P("mp", "dp"),
            P("dp", None, "mp"),
            P("dp", None, "mp"),
            P("mp", "dp"),
            P("mp", "dp"),
            P("dp", "mp"),
            P("dp", "mp"),
            P("mp", "dp"),
            P("mp", "dp"),
            P(),
            P(),
            P(),
        ),
        out_specs=(
            P(None, ("dp", "mp"), None, None),
            P(None, ("dp", "mp"), None, None),
            P("dp", None, "mp"),
            P("dp", None, "mp"),
            P("dp", None, "mp"),
            P("dp", None, "mp"),
            P("dp", None, "mp"),
            P("mp", "dp"),
            P("mp", "dp"),
            P("mp", "dp"),
            P("mp", "dp"),
            P("mp", "dp"),
            P("dp", "mp"),
            P("dp", "mp"),
            P("dp", "mp"),
            P("dp", "mp"),
            P("dp", "mp"),
            P("mp", "dp"),
            P("mp", "dp"),
            P("mp", "dp"),
            P("mp", "dp"),
            P("mp", "dp"),
            P(),
            P(),
            P(),
            P(),
            P(),
        ),
        check_vma=False,
    )
```

profile of v0, /device:TPU:0, one launch (start us, length us, event | category | flops | bytes accessed | tf_op | source)
XLA Modules:
  0.0 1116.6 jit_solution(12952515650628165163)
XLA Ops:
  17.6 49.4 %all_gather.45 = bf16[384,768]{0,1:T(8,128)(2,1)} all-gather(bf16[384,48]{0,1:T(8,128)(2,1)S(1)} %convert_element_type.246), channel_id=1, replica_groups=mesh['dp'=16,'mp'=2] {'dp'}, dimensions={1}, use_global_device_ids=true | all-gather | bytes 626688 | tf_op jit(solution)/shard_map/all_gather | solution.py:119
  67.0 7.5 all-gather.16.cloned.1.call-done
  77.1 7.6 all-gather.34.cloned.1.call-done
  90.4 7.3 all-gather.36.cloned.1.call-done
  159.8 10.2 reduce-scatter.17.cloned.1.call-done
  176.8 60.0 %all-gather.20.cloned.1.call-done = bf16[768,1536]{1,0:T(8,128)(2,1)} async-done(((bf16[48,1536]{1,0:T(8,128)(2,1)}), bf16[768,1536]{1,0:T(8,128)(2,1)}) %all-gather.20.cloned.1.call-update) | async-done | bytes 2359312 | tf_op jit(solution)/shard_map/all_gather | solution.py:118
  236.7 10.6 all-gather.24.cloned.1.call-done
  247.3 7.1 fusion.121
  254.4 5.9 all-gather.18.cloned.1.call-done
  260.3 31.8 %multiply_convert_fusion.3 = (bf16[960,1536]{1,0:T(8,128)(2,1)}, f32[960,1536]{1,0:T(8,128)}, bf16[960,1536]{1,0:T(8,128)(2,1)}, f32[960,1536]{1,0:T(8,128)}, f32[960,1536]{1,0:T(8,128)}) fusion(f32[1536]{0:T(1024)S(1)} %dynamic_slice.11, f32[960,1536]{1,0:T(8,128)} %fusion.121, bf16[960,768]{1,0:T(8,128)(2,1)} %bitcast.248, ...), kind=kOutput, calls=%fused_computation.30 | convolution fusion | flops 2459566080 | bytes 33331200 | tf_op jit(solution)/shard_map/dot_general | solution.py:177
  292.1 35.1 %all-gather.22.cloned.1.call-done = bf16[1536,768]{0,1:T(8,128)(2,1)} async-done(((bf16[1536,48]{0,1:T(8,128)(2,1)}), bf16[1536,768]{0,1:T(8,128)(2,1)}) %all-gather.22.cloned.1.call-update) | async-done | bytes 2359312 | tf_op jit(solution)/shard_map/all_gather | solution.py:120
  327.2 6.7 fusion.120
  333.9 6.6 fusion.122
  343.4 14.2 %reduce-scatter.19.cloned.1.call-done = f32[3,160,768]{2,1,0:T(8,128)} async-done(((f32[6,160,768]{2,1,0:T(8,128)}), f32[3,160,768]{2,1,0:T(8,128)}) %reduce-scatter.19.cloned.1.call-update) | async-done | bytes 1474576 | tf_op jit(solution)/shard_map/reduce_scatter | solution.py:183
  368.6 10.1 all-gather.30.cloned.1.call-done
  378.7 7.0 fusion.124
  385.8 5.4 all-gather.26.cloned.1.call-done
  391.2 16.5 %convert_reduce_fusion.1 = (f32[1536]{0:T(1024)}, bf16[960,1536]{1,0:T(8,128)(2,1)S(1)}, f32[1536]{0:T(1024)}, bf16[960,1536]{1,0:T(8,128)(2,1)}) fusion(f32[960,1536]{1,0:T(8,128)} %get-tuple-element.100, f32[960,1536]{1,0:T(8,128)} %get-tuple-element.157, f32[1536]{0:T(1024)S(1)} %dynamic_slice.11, f32[960,1536]{1,0:T(8,128)} %fusion.124, ...), kind=kOutput, calls=%fused_computation.5 | convolution fusion | flops 2315056128 | bytes 39241728 | tf_op jit(solution)/shard_map/dot_general | solution.py:53
  407.7 4.0 fusion.123
  411.8 6.6 fusion.125
  418.5 5.1 reduce-scatter.21.cloned.1.call-done
  423.6 5.0 multiply_reduce_fusion.3
  428.7 9.0 reduce-scatter.25.cloned.1.call-done
  437.7 4.8 multiply_reduce_fusion.2
  446.0 5.1 fusion.129
  451.1 4.4 convolution_add_fusion.1
  456.8 4.7 fusion.128
  461.5 4.5 convolution_add_fusion.2
  487.9 6.1 convert_reduce_fusion.2
  493.9 4.7 multiply_reduce_fusion
  511.9 6.3 multiply_convert_fusion
  539.6 5.7 copy.163
  545.2 6.6 dot_general.154
  551.8 5.3 convolution_convert_fusion
  557.5 4.6 convert_reduce_fusion.4
  567.7 5.4 multiply_reduce_fusion.1
  593.5 5.7 copy.149
  599.2 6.7 dot_general.145
  605.9 4.8 convolution_convert_fusion.1
  611.1 4.2 fusion.126
  615.3 5.5 convolution_add_fusion
  620.8 5.2 copy.165
  661.5 93.8 %reduce-scatter.33.cloned.1.call-done = f32[48,1536]{1,0:T(8,128)} async-done(((f32[768,1536]{1,0:T(8,128)}), f32[48,1536]{1,0:T(8,128)}) %reduce-scatter.33.cloned.1.call-update) | async-done | bytes 294928 | tf_op jit(solution)/shard_map/reduce_scatter | solution.py:73
  758.0 124.8 %reduce-scatter.31.cloned.1.call-done = f32[384,48]{0,1:T(8,128)} async-done(((f32[384,768]{0,1:T(8,128)}), f32[384,48]{0,1:T(8,128)}) %reduce-scatter.31.cloned.1.call-update) | async-done | bytes 73744 | tf_op jit(solution)/shard_map/reduce_scatter | solution.py:74
  885.1 8.1 reduce-scatter.27.cloned.1.call-done
  893.1 13.0 %reduce-scatter.23.cloned.1.call-done = bf16[3,160,768]{2,1,0:T(8,128)(2,1)} async-done(((bf16[6,160,768]{2,1,0:T(8,128)(2,1)}), bf16[3,160,768]{2,1,0:T(8,128)(2,1)}) %reduce-scatter.23.cloned.1.call-update) | async-done | bytes 737296 | tf_op jit(solution)/shard_map/reduce_scatter | solution.py:248
  910.1 136.2 %reduce-scatter.29.cloned.1.call-done = f32[48,3,384]{2,0,1:T(8,128)} async-done(((f32[768,3,384]{2,0,1:T(8,128)}), f32[48,3,384]{2,0,1:T(8,128)}) %reduce-scatter.29.cloned.1.call-update) | async-done | bytes 221200 | tf_op jit(solution)/shard_map/reduce_scatter | solution.py:72
  1057.7 40.6 %all-reduce.2 = (f32[4]{0:T(128)S(1)}, f32[4]{0:T(128)S(1)}, f32[12,768]{1,0:T(8,128)S(1)}) all-reduce(f32[4]{0:T(128)S(1)} %pad_maximum_fusion.3, f32[4]{0:T(128)S(1)} %pad_maximum_fusion.4, f32[12,768]{1,0:T(8,128)S(1)} %copy-done.61), channel_id=1, replica_groups=mesh['dp'=16,'mp'=2] {'dp','mp'}, use_global_device_ids=true, to_apply=%region_35.36 | all-reduce | flops 9224 | bytes 73792 | tf_op jit(solution)/shard_map/psum | solution.py:294
  (421 shorter events, 249.6 us)
Async XLA Ops:
  7.2 67.3 %all-gather.16.cloned.1.call-start = ((), (), s32[]{:S(2)}) async-start(), calls=%async_computation.12 | async-start | bytes 1880064 | tf_op jit(solution)/shard_map/all_gather | solution.py:117
  8.9 75.8 %all-gather.34.cloned.1.call-start = ((), (), s32[]{:S(2)}) async-start(), calls=%async_computation.33 | async-start | bytes 2211840 | tf_op jit(solution)/shard_map/all_gather | solution.py:134
  11.5 86.1 %all-gather.36.cloned.1.call-start = ((), (), s32[]{:S(2)}) async-start(), calls=%async_computation.34 | async-start | bytes 2211840 | tf_op jit(solution)/shard_map/all_gather | solution.py:134
  12.3 147.5 %reduce-scatter.13.cloned.1.call-start = ((), (), s32[]{:S(2)}) async-start(), calls=%async_computation.13 | async-start | bytes 4423680 | tf_op jit(solution)/shard_map/reduce_scatter | solution.py:170
  77.1 20.6 %copy-start.39 = (bf16[768,3,384]{0,2,1:T(8,128)(2,1)}, bf16[768,3,384]{0,2,1:T(8,128)(2,1)S(1)}, u32[]{:S(2)}) copy-start(bf16[768,3,384]{0,2,1:T(8,128)(2,1)S(1)} %copy.119) | copy-start | bytes 5308420
  129.4 18.8 %copy-start.21 = (bf16[6,160,6,64]{1,0,3,2:T(8,128)(2,1)}, bf16[6,160,6,64]{1,0,3,2:T(8,128)(2,1)S(1)}, u32[]{:S(2)}) copy-start(bf16[6,160,6,64]{1,0,3,2:T(8,128)(2,1)S(1)} %get-tuple-element.138) | copy-start | bytes 2211844
  142.4 27.5 %reduce-scatter.17.cloned.1.call-start = ((), (), s32[]{:S(2)}) async-start(), calls=%async_computation.18 | async-start | bytes 4423680 | tf_op jit(solution)/shard_map/reduce_scatter | solution.py:170
  158.0 78.7 %all-gather.20.cloned.1.call-start = ((), (), s32[]{:S(2)}) async-start(), calls=%async_computation.15 | async-start | bytes 2506752 | tf_op jit(solution)/shard_map/all_gather | solution.py:118
  159.7 87.7 %all-gather.24.cloned.1.call-start = ((), (), s32[]{:S(2)}) async-start(), calls=%async_computation.19 | async-start | bytes 2211840 | tf_op jit(solution)/shard_map/all_gather | solution.py:174
  172.7 269.8 %copy-start.2 = (f32[3,160,768]{2,1,0:T(8,128)}, f32[3,160,768]{2,1,0:T(8,128)S(1)}, u32[]{:S(2)}) copy-start(f32[3,160,768]{2,1,0:T(8,128)S(1)} %get-tuple-element.118) | copy-start | bytes 4423684
  173.4 269.1 %copy-start.64 = (f32[3,160]{1,0:T(4,128)}, f32[3,160]{1,0:T(4,128)S(1)}, u32[]{:S(2)}) copy-start(f32[3,160]{1,0:T(4,128)S(1)} %add_rsqrt_fusion.3) | copy-start | bytes 5764
  175.1 85.2 %all-gather.18.cloned.1.call-start = ((), (), s32[]{:S(2)}) async-start(), calls=%async_computation.14 | async-start | bytes 2211840 | tf_op jit(solution)/shard_map/all_gather | solution.py:174
  175.8 151.4 %all-gather.22.cloned.1.call-start = ((), (), s32[]{:S(2)}) async-start(), calls=%async_computation.16 | async-start | bytes 2506752 | tf_op jit(solution)/shard_map/all_gather | solution.py:120
  176.6 166.8 %reduce-scatter.15.cloned.1.call-start = ((), (), s32[]{:S(2)}) async-start(), calls=%async_computation.17 | async-start | bytes 4423680 | tf_op jit(solution)/shard_map/reduce_scatter | solution.py:183
  333.9 23.7 %reduce-scatter.19.cloned.1.call-start = ((), (), s32[]{:S(2)}) async-start(), calls=%async_computation.20 | async-start | bytes 4423680 | tf_op jit(solution)/shard_map/reduce_scatter | solution.py:183
  340.5 17.1 %copy-start.74 = (f32[768]{0:T(1024)S(1)}, f32[768]{0:T(1024)}, u32[]{:S(2)}) copy-start(f32[768]{0:T(1024)} %get-tuple-element.54) | copy-start | bytes 9220
  340.6 38.2 %all-gather.30.cloned.1.call-start = ((), (), s32[]{:S(2)}) async-start(), calls=%async_computation.25 | async-start | bytes 2211840 | tf_op jit(solution)/shard_map/all_gather | solution.py:191
  367.7 23.5 %all-gather.26.cloned.1.call-start = ((), (), s32[]{:S(2)}) async-start(), calls=%async_computation.21 | async-start | bytes 2211840 | tf_op jit(solution)/shard_map/all_gather | solution.py:191
  368.4 55.2 %reduce-scatter.21.cloned.1.call-start = ((), (), s32[]{:S(2)}) async-start(), calls=%async_computation.22 | async-start | bytes 4423680 | tf_op jit(solution)/shard_map/reduce_scatter | solution.py:197
  391.1 16.5 %copy-start.87 = (bf16[768,1536]{1,0:T(8,128)(2,1)S(1)}, bf16[768,1536]{1,0:T(8,128)(2,1)}, u32[]{:S(2)}) copy-start(bf16[768,1536]{1,0:T(8,128)(2,1)} %all-gather.20.cloned.1.call-done) | copy-start | bytes 7077892
  411.8 25.9 %reduce-scatter.25.cloned.1.call-start = ((), (), s32[]{:S(2)}) async-start(), calls=%async_computation.26 | async-start | bytes 4423680 | tf_op jit(solution)/shard_map/reduce_scatter | solution.py:197
  418.4 56.8 %all-gather.32.cloned.1.call-start = ((), (), s32[]{:S(2)}) async-start(), calls=%async_computation.27 | async-start | bytes 2211840 | tf_op jit(solution)/shard_map/all_gather | solution.py:202
  428.7 13.9 %copy-start.70 = (f32[3,160]{1,0:T(4,128)}, f32[3,160]{1,0:T(4,128)S(1)}, u32[]{:S(2)}) copy-start(f32[3,160]{1,0:T(4,128)S(1)} %broadcast_multiply_fusion.4) | copy-start | bytes 5764
  428.7 13.9 %copy-start.71 = (f32[3,160]{1,0:T(4,128)}, f32[3,160]{1,0:T(4,128)S(1)}, u32[]{:S(2)}) copy-start(f32[3,160]{1,0:T(4,128)S(1)} %broadcast_multiply_fusion.5) | copy-start | bytes 5764
  445.1 37.8 %all-gather.28.cloned.1.call-start = ((), (), s32[]{:S(2)}) async-start(), calls=%async_computation.23 | async-start | bytes 2211840 | tf_op jit(solution)/shard_map/all_gather | solution.py:202
  445.7 213.0 %reduce-scatter.35.cloned.1.call-start = ((), (), s32[]{:S(2)}) async-start(), calls=%async_computation.32 | async-start | bytes 5013504 | tf_op jit(solution)/shard_map/reduce_scatter | solution.py:75
  455.5 299.7 %reduce-scatter.33.cloned.1.call-start = ((), (), s32[]{:S(2)}) async-start(), calls=%async_computation.31 | async-start | bytes 5013504 | tf_op jit(solution)/shard_map/reduce_scatter | solution.py:73
  466.0 416.8 %reduce-scatter.31.cloned.1.call-start = ((), (), s32[]{:S(2)}) async-start(), calls=%async_computation.30 | async-start | bytes 1253376 | tf_op jit(solution)/shard_map/reduce_scatter | solution.py:74
  498.6 394.5 %reduce-scatter.27.cloned.1.call-start = ((), (), s32[]{:S(2)}) async-start(), calls=%async_computation.28 | async-start | bytes 2211840 | tf_op jit(solution)/shard_map/reduce_scatter | solution.py:248
  505.4 52.1 %copy-start.14 = (bf16[6,160,6,64]{1,3,2,0:T(8,128)(2,1)}, bf16[6,160,6,64]{1,3,2,0:T(8,128)(2,1)S(1)}, u32[]{:S(2)}) copy-start(bf16[6,160,6,64]{1,3,2,0:T(8,128)(2,1)S(1)} %copy.138) | copy-start | bytes 2211844
  557.2 349.0 %reduce-scatter.23.cloned.1.call-start = ((), (), s32[]{:S(2)}) async-start(), calls=%async_computation.24 | async-start | bytes 2211840 | tf_op jit(solution)/shard_map/reduce_scatter | solution.py:248
  610.7 435.6 %reduce-scatter.29.cloned.1.call-start = ((), (), s32[]{:S(2)}) async-start(), calls=%async_computation.29 | async-start | bytes 3760128 | tf_op jit(solution)/shard_map/reduce_scatter | solution.py:72
  627.4 31.3 %copy-start.35 = (f32[1536,48]{0,1:T(8,128)S(1)}, f32[1536,48]{0,1:T(8,128)}, u32[]{:S(2)}) copy-start(f32[1536,48]{0,1:T(8,128)} %param.24) | copy-start | bytes 884740
  636.4 118.9 %copy-start.37 = (f32[48,1536]{1,0:T(8,128)S(1)}, f32[48,1536]{1,0:T(8,128)}, u32[]{:S(2)}) copy-start(f32[48,1536]{1,0:T(8,128)} %param.23) | copy-start | bytes 884740
  639.0 267.2 %copy-start.3 = (f32[3,160,768]{2,1,0:T(8,128)S(1)}, f32[3,160,768]{2,1,0:T(8,128)}, u32[]{:S(2)}) copy-start(f32[3,160,768]{2,1,0:T(8,128)} %copy-done.2) | copy-start | bytes 4423684
  1048.4 58.4 %copy-start.47 = (f32[48,3,384]{2,0,1:T(8,128)}, f32[48,3,384]{2,0,1:T(8,128)S(1)}, u32[]{:S(2)}) copy-start(f32[48,3,384]{2,0,1:T(8,128)S(1)} %get-tuple-element.87) | copy-start | bytes 663556
  1048.4 58.4 %copy-start.48 = (f32[48,3,384]{2,0,1:T(8,128)}, f32[48,3,384]{2,0,1:T(8,128)S(1)}, u32[]{:S(2)}) copy-start(f32[48,3,384]{2,0,1:T(8,128)S(1)} %get-tuple-element.88) | copy-start | bytes 663556
  1053.8 51.7 %copy-start.50 = (f32[384,48]{0,1:T(8,128)S(1)}, f32[384,48]{0,1:T(8,128)}, u32[]{:S(2)}) copy-start(f32[384,48]{0,1:T(8,128)} %param.22) | copy-start | bytes 221188
  1053.8 51.7 %copy-start.55 = (f32[384,48]{0,1:T(8,128)S(1)}, f32[384,48]{0,1:T(8,128)}, u32[]{:S(2)}) copy-start(f32[384,48]{0,1:T(8,128)} %get-tuple-element.89) | copy-start | bytes 221188
  1053.8 51.7 %copy-start.56 = (f32[384,48]{0,1:T(8,128)S(1)}, f32[384,48]{0,1:T(8,128)}, u32[]{:S(2)}) copy-start(f32[384,48]{0,1:T(8,128)} %get-tuple-element.90) | copy-start | bytes 221188
  1053.8 52.4 %copy-start.63 = (f32[12,768]{1,0:T(8,128)S(1)}, f32[12,768]{1,0:T(8,128)}, u32[]{:S(2)}) copy-start(f32[12,768]{1,0:T(8,128)} %param.33) | copy-start | bytes 110596
  1053.8 52.4 %copy-start.66 = (f32[12,768]{1,0:T(8,128)S(1)}, f32[12,768]{1,0:T(8,128)}, u32[]{:S(2)}) copy-start(f32[12,768]{1,0:T(8,128)} %param.35) | copy-start | bytes 110596
  1053.8 52.4 %copy-start.67 = (f32[12,768]{1,0:T(8,128)S(1)}, f32[12,768]{1,0:T(8,128)}, u32[]{:S(2)}) copy-start(f32[12,768]{1,0:T(8,128)} %param.34) | copy-start | bytes 110596
  1053.8 53.1 %copy-start.38 = (f32[48,3,384]{2,0,1:T(8,128)S(1)}, f32[48,3,384]{2,0,1:T(8,128)}, u32[]{:S(2)}) copy-start(f32[48,3,384]{2,0,1:T(8,128)} %param.21) | copy-start | bytes 663556
  1053.8 53.9 %copy-start.43 = (f32[1536,48]{0,1:T(8,128)S(1)}, f32[1536,48]{0,1:T(8,128)}, u32[]{:S(2)}) copy-start(f32[1536,48]{0,1:T(8,128)} %get-tuple-element.93) | copy-start | bytes 884740
  1053.8 53.9 %copy-start.44 = (f32[1536,48]{0,1:T(8,128)S(1)}, f32[1536,48]{0,1:T(8,128)}, u32[]{:S(2)}) copy-start(f32[1536,48]{0,1:T(8,128)} %get-tuple-element.94) | copy-start | bytes 884740
  1057.7 50.9 %copy-start.45 = (f32[48,1536]{1,0:T(8,128)S(1)}, f32[48,1536]{1,0:T(8,128)}, u32[]{:S(2)}) copy-start(f32[48,1536]{1,0:T(8,128)} %get-tuple-element.91) | copy-start | bytes 884740
  1057.7 50.9 %copy-start.46 = (f32[48,1536]{1,0:T(8,128)S(1)}, f32[48,1536]{1,0:T(8,128)}, u32[]{:S(2)}) copy-start(f32[48,1536]{1,0:T(8,128)} %get-tuple-element.92) | copy-start | bytes 884740
  (75 other events, 334.0 us)
Sparse Core Ops, SparseCore 0:
  11.3 63.1 all-gather.15
  76.6 8.0 all-gather.33
  86.8 10.8 all-gather.35
  142.6 11.7 reduce-scatter.12
  158.2 11.7 reduce-scatter.16
  173.2 63.5 all-gather.19
  238.8 8.4 all-gather.23
  249.5 10.8 all-gather.17
  263.7 63.4 all-gather.21
  334.0 9.3 reduce-scatter.14
  345.8 11.8 reduce-scatter.18
  367.8 10.9 all-gather.29
  380.3 10.8 all-gather.25
  411.9 11.6 reduce-scatter.20
  425.8 11.8 reduce-scatter.24
  445.2 10.9 all-gather.31
  457.6 10.8 all-gather.27
  474.1 138.5 reduce-scatter.34
  619.2 135.9 reduce-scatter.32
  760.4 122.3 reduce-scatter.30
  885.0 8.0 reduce-scatter.26
  896.0 10.1 reduce-scatter.22
  911.8 134.4 reduce-scatter.28
where the time goes:
time: 1130 us; the launch traced here: 1120 us
  waiting for transfers between devices  569 us (50%)
  matrix products  184 us (16%)
  local copies, waits for them, and re-layouts  171 us (15%)
  blocking collectives  92.6 us (8%)
  other arithmetic  76.1 us (7%)
  between operations  21.8 us (2%)
    reduce_scatter x1, waiting for transfers between devices, reduce_weights(): lax.psum_scatter(local_grads[0], 'dp', scatter_dimension=0, tiled=True)  136 us
    reduce_scatter x1, waiting for transfers between devices, reduce_weights(): lax.psum_scatter(local_grads[2], 'dp', scatter_dimension=1, tiled=True)  125 us
    reduce_scatter x1, waiting for transfers between devices, reduce_weights(): lax.psum_scatter(local_grads[1], 'dp', scatter_dimension=0, tiled=True)  93.8 us
    all_gather x1, waiting for transfers between devices, body(): lax.all_gather(ffn_in.astype(jnp.bfloat16), 'dp', axis=0, tiled=True)  60 us
    dot_general x8, matrix products, times_transposed(): lax.dot_general(left, right, (((1,), (1,)), ((), ())), preferred_element_...  50.1 us
    all_gather x1, blocking collectives, body(): lax.all_gather(attn_out.astype(jnp.bfloat16), 'dp', axis=1, tiled=True)  49.4 us
    psum x1, blocking collectives, body(): lax.psum((weight_squares, step_squares), ('dp', 'mp'))  40.6 us
    dot_general x2, matrix products, body(): jnp.dot(ffn_rows, w_up, preferred_element_type=jnp.float32) + bias_upper  38.9 us
  transfers between devices with their start and end apart: 23, of which 19 were waited for; matrix products, arithmetic and copies ran while one was open for 28% of the time, Pallas kernels for 0%

commit v1 on v0

v1 whole, which is shorter than its diff:
```python
import functools

import jax
import jax.numpy as jnp
from jax import lax
from jax.experimental import pallas as pl
from jax.experimental.pallas import tpu as pltpu
from jax.sharding import PartitionSpec as P

HEAD = 64
STEP = 10
NORM_EPS = 1e-05
RATE_MATRIX = 0.3
RATE_VECTOR = 0.2
BETA_FIRST = 0.9
BETA_SECOND = 0.999
ADAM_EPS = 1e-06
DECAY_RATE = 0.01
MASKED_SCORE = -1000000000.0

MESH = pl.DeviceIdType.MESH
bf16, f32 = jnp.bfloat16, jnp.float32
UNITS = 12
HALF = 384
WIDE = 768
LANES = 128
QUAD = 256
BLOCK = 32
ROWS = 320


def nn(left, right):
    return lax.dot_general(left, right, (((1,), (0,)), ((), ())), preferred_element_type=f32)


def nt(left, right):
    return lax.dot_general(left, right, (((1,), (1,)), ((), ())), preferred_element_type=f32)


def tn(left, right):
    return lax.dot_general(left, right, (((0,), (0,)), ((), ())), preferred_element_type=f32)


def tile(index, size):
    return pl.ds(pl.multiple_of(index * size, size), size)


def loop(count, body):
    def step(index, carry):
        body(index)
        return carry

    lax.fori_loop(0, count, step, 0)


def mean_last(values):
    return jnp.sum(values, axis=-1, keepdims=True) * (1.0 / values.shape[-1])


def fold_rows(values):
    return jnp.sum(values.reshape(values.shape[0] // 8, 8, values.shape[1]), axis=0)


def head_lane():
    return lax.broadcasted_iota(jnp.int32, (1, QUAD), 1) // HEAD


def spread_heads(values):
    lane = head_lane()
    zero = jnp.zeros_like(values)
    return jnp.concatenate([jnp.where(lane == head, values, zero) for head in range(4)], axis=0)


def pick_heads(values, length):
    lane = head_lane()
    result = values[:length]
    for head in range(1, 4):
        result = jnp.where(lane == head, values[head * length : (head + 1) * length], result)
    return result


def pair(ref, rows, offset):
    return jnp.concatenate(
        [ref[rows, pl.ds(offset, LANES)], ref[rows, pl.ds(HALF + offset, LANES)]], axis=1
    )


def put_pair(ref, rows, offset, values):
    ref[rows, pl.ds(offset, LANES)] = values[:, :LANES]
    ref[rows, pl.ds(HALF + offset, LANES)] = values[:, LANES:]


def main_kernel(
    comm,
    lengths,
    tokens_hbm,
    cot_hbm,
    small,
    w_in,
    w_mid,
    w_up,
    w_down,
    *rest,
):
    if not comm:
        whole_hbm, *rest = rest
    (
        out_hbm,
        back,
        shard,
        vectors,
        probs_hbm,
        unit,
        packed,
        context,
        normed,
        inverse,
        first,
        hidden,
        slope,
        own,
        cot,
        flip_a,
        flip_b,
        probs,
        sums,
        up_sums,
        local_sem,
        probs_sem,
        *rest,
    ) = rest
    if comm:
        (sib_in, diag_in, line_in, z_in, send, recv, rs_send, rs_recv) = rest
    micro, per_micro = lengths.shape
    chains = micro * per_micro
    length = own.shape[0] // chains
    count = own.shape[0]

    planes = unit.shape[1]
    if comm:
        rank = lax.axis_index("dp")
        core = lax.axis_index("mp")
        z, y, x = rank // 4, (rank // 2) % 2, rank % 2
        mine = pl.ds(pl.multiple_of(core * HALF, HALF), HALF)
        other = pl.ds(pl.multiple_of((1 - core) * HALF, HALF), HALF)

        def device(zz, yy, xx, cc):
            return (zz * 4 + yy * 2 + xx, cc)

        y1, x1 = jnp.where(core == 0, y, 1 - y), jnp.where(core == 0, 1 - x, x)
        y2, x2 = jnp.where(core == 0, 1 - y, y), jnp.where(core == 0, x, 1 - x)
        near = device(z, y1, x1, core)
        next_ = device(z, y2, x2, core)
        sibling = device(z, y, x, 1 - core)

        def plane(step):
            return lax.rem(z + step, planes)

        def plane_back(step):
            return lax.rem(z + planes - step, planes)

        def remote(src, dst, ssem, rsem, target):
            return pltpu.make_async_remote_copy(
                src_ref=src,
                dst_ref=dst,
                send_sem=ssem,
                recv_sem=rsem,
                device_id=target,
                device_id_type=MESH,
            )

        LINE = planes - 1

        def gz(u, step):
            piece = unit.at[u, z, y, x, :, mine]
            return remote(
                piece, piece, send.at[u, step - 1], recv.at[u, step - 1], device(plane(step), y, x, core)
            )

        def gline(u, which):
            piece = unit.at[u, :, y, x, :, mine]
            return remote(
                piece,
                piece,
                send.at[u, LINE + which],
                recv.at[u, LINE + which],
                near if which else next_,
            )

        def gdiag(u):
            piece = unit.at[u, :, y2, x2, :, mine]
            return remote(piece, piece, send.at[u, LINE + 2], recv.at[u, LINE + 2], near)

        def gsib(u):
            piece = unit.at[u, :, :, :, :, mine]
            return remote(piece, piece, send.at[u, LINE + 3], recv.at[u, LINE + 3], sibling)

        def ag_z(u):
            for step in range(1, planes):
                gz(u, step).start()

        def ag_line(u):
            for step in range(1, planes):
                gz(u, step).wait_recv()
            gline(u, 0).start()
            gline(u, 1).start()

        def ag_diag(u):
            gline(u, 0).wait_recv()
            gdiag(u).start()

        def ag_sib(u):
            gline(u, 1).wait_recv()
            gdiag(u).wait_recv()
            gsib(u).start()

        def ag_ready(u):
            gsib(u).wait_recv()

        def ag_sent(u):
            for step in range(1, planes):
                gz(u, step).wait_send()
            gline(u, 0).wait_send()
            gline(u, 1).wait_send()
            gdiag(u).wait_send()
            gsib(u).wait_send()

        def rsib(u):
            return remote(
                unit.at[u, :, :, :, :, other], sib_in.at[u], rs_send.at[u, 0], rs_recv.at[u, 0], sibling
            )

        def rdiag(u):
            return remote(
                unit.at[u, :, 1 - y, 1 - x, :, mine],
                diag_in.at[u],
                rs_send.at[u, 1],
                rs_recv.at[u, 1],
                near,
            )

        def rline(u, which):
            yy, xx = (y2, x2) if which else (y1, x1)
            return remote(
                unit.at[u, :, yy, xx, :, mine],
                line_in.at[u, which],
                rs_send.at[u, 2 + which],
                rs_recv.at[u, 2 + which],
                next_ if which else near,
            )

        def rz(u, step):
            return remote(
                unit.at[u, plane(step), y, x, :, mine],
                z_in.at[u, step - 1],
                rs_send.at[u, 3 + step],
                rs_recv.at[u, 3 + step],
                device(plane(step), y, x, core),
            )

        def rs_start(u):
            rsib(u).start()

        def rs_own(u):
            rsib(u).wait_recv()

            def add(zz):
                for yy in range(2):
                    for xx in range(2):
                        unit[u, zz, yy, xx, :, mine] = (
                            unit[u, zz, yy, xx, :, mine].astype(f32) + sib_in[u, zz, yy, xx].astype(f32)
                        ).astype(bf16)

            loop(planes, add)
            rdiag(u).start()
            rline(u, 0).start()

        def rs_diag(u):
            rdiag(u).wait_recv()

            def add(zz):
                unit[u, zz, y2, x2, :, mine] = (
                    unit[u, zz, y2, x2, :, mine].astype(f32) + diag_in[u, zz].astype(f32)
                ).astype(bf16)

            loop(planes, add)
            rline(u, 1).start()

        def rs_line(u):
            rline(u, 0).wait_recv()
            rline(u, 1).wait_recv()

            def add(zz):
                unit[u, zz, y, x, :, mine] = (
                    unit[u, zz, y, x, :, mine].astype(f32)
                    + line_in[u, 0, zz].astype(f32)
                    + line_in[u, 1, zz].astype(f32)
                ).astype(bf16)

            loop(planes, add)
            for step in range(1, planes):
                rz(u, step).start()

        def rs_done(u):
            total = unit[u, z, y, x, :, mine].astype(f32)
            for step in range(1, planes):
                rz(u, step).wait_recv()
                total = total + z_in[u, step - 1].astype(f32)
            shard[u] = total

        def rs_sent(u):
            rsib(u).wait_send()
            rdiag(u).wait_send()
            rline(u, 0).wait_send()
            rline(u, 1).wait_send()
            for step in range(1, planes):
                rz(u, step).wait_send()

    def pump(t):
        if not comm:
            return
        if 0 <= t + 3 < UNITS:
            ag_z(t + 3)
        if 0 <= t + 2 < UNITS:
            ag_line(t + 2)
        if 0 <= t + 1 < UNITS:
            ag_diag(t + 1)
        if 0 <= t < UNITS:
            ag_sib(t)

    def ready(u):
        if comm:
            ag_ready(u)

    def weights(u):
        return unit[u].reshape(WIDE, WIDE)

    def unit_cols(u, columns):
        return unit[u, :, :, :, :, columns].reshape(WIDE, columns.size)

    own_copy = pltpu.make_async_copy(tokens_hbm, own, local_sem.at[0])
    cot_copy = pltpu.make_async_copy(cot_hbm, cot, local_sem.at[1])
    out_copy = pltpu.make_async_copy(cot, out_hbm, local_sem.at[2])
    own_copy.start()
    cot_copy.start()

    if comm:
        barrier = pltpu.get_barrier_semaphore()
        greeted = [device(plane(step), y, x, core) for step in range(1, planes)]
        greeted += [near, next_, sibling]
        for target in greeted:
            pl.semaphore_signal(barrier, inc=1, device_id=target, device_id_type=MESH)
        for g in range(3):
            for kind in range(3):
                columns = pl.ds(pl.multiple_of(core * HALF + kind * LANES, LANES), LANES)
                unit[g, z, y, x, :, columns] = w_in[:, kind, pl.ds(g * LANES, LANES)].astype(bf16)
        unit[3, z, y, x, :, mine] = w_mid[...].T.astype(bf16)
        for u in range(4):
            unit[4 + u, z, y, x, :, mine] = w_up[:, pl.ds(u * HALF, HALF)].astype(bf16)
            unit[8 + u, z, y, x, :, mine] = w_down[pl.ds(u * HALF, HALF), :].T.astype(bf16)
        pl.semaphore_wait(barrier, len(greeted))
    else:
        unit_copy = pltpu.make_async_copy(whole_hbm, unit, local_sem.at[3])
        unit_copy.start()
        unit_copy.wait()

    pump(-3)
    sums[...] = jnp.zeros_like(sums)
    up_sums[...] = jnp.zeros_like(up_sums)
    pump(-2)
    own_copy.wait()
    pump(-1)
    pump(0)

    def probs_out(t):
        return pltpu.make_async_copy(probs.at[t % 2], probs_hbm.at[t], probs_sem.at[t % 2])

    def probs_back(t):
        return pltpu.make_async_copy(probs_hbm.at[t], probs.at[t % 2], probs_sem.at[t % 2])

    position = lax.broadcasted_iota(jnp.int32, (1, length), 1)

    for g in range(3):
        ready(g)
        bias = jnp.concatenate(
            [
                piece
                for c in range(2)
                for piece in (
                    small[pl.ds(0, 1), pl.ds(c * HALF + g * LANES, LANES)],
                    jnp.zeros((1, LANES), f32),
                    small[pl.ds(1, 1), pl.ds(c * HALF + g * LANES, LANES)],
                )
            ],
            axis=1,
        )
        lane = lax.broadcasted_iota(jnp.int32, (1, WIDE), 1) % HALF
        scale = jnp.where(lane < LANES, HEAD ** (-0.5), 1.0)

        def project(r):
            rows = tile(r, ROWS)
            for j in range(3):
                cols = pl.ds(j * QUAD, QUAD)
                part = slice(j * QUAD, (j + 1) * QUAD)
                packed[g, rows, cols] = (
                    (nn(own[rows, :], unit_cols(g, cols)) + bias[:, part]).astype(bf16).astype(f32)
                    * scale[:, part]
                ).astype(bf16)

        loop(count // ROWS, project)
        pump(1 + 2 * g)

        def attend(chain):
            t = g * chains + chain

            @pl.when(t >= 2)
            def _():
                probs_out(t - 2).wait()

            rows = tile(chain, length)
            here = packed.at[g]
            queries = spread_heads(pair(here, rows, 0))
            keys = pair(here, rows, LANES)
            values = pair(here, rows, 2 * LANES)
            limit = lengths[chain // per_micro, chain % per_micro]
            scores = jnp.where(position < limit, nt(queries, keys), MASKED_SCORE)
            peak = jnp.max(scores, axis=1, keepdims=True)
            exponent = jnp.exp(scores - peak)
            total = jnp.sum(exponent, axis=1, keepdims=True)
            low = (exponent * (1.0 / total)).astype(bf16)
            probs[t % 2] = low
            probs_out(t).start()
            mixed = pick_heads(nn(low, values), length).astype(bf16)
            put_pair(context, rows, g * LANES, mixed)

        def attend_first(chain):
            attend(chain)

        def attend_second(chain):
            attend(chain + chains // 2)

        loop(chains // 2, attend_first)
        pump(2 + 2 * g)
        loop(chains - chains // 2, attend_second)

    ready(3)

    def mid(r):
        rows = tile(r, ROWS)
        back[rows, :] = nt(context[rows, :], weights(3))

    loop(count // ROWS, mid)

    def first_norm(r):
        rows = tile(r, BLOCK)
        value = own[rows, :].astype(f32) + back[rows, :] + small[pl.ds(2, 1), :]
        center = value - mean_last(value)
        root = lax.rsqrt(mean_last(center * center) + NORM_EPS)
        scaled = center * root
        normed[rows, :] = scaled
        inverse[rows, :] = root
        first[rows, :] = (scaled * small[pl.ds(3, 1), :] + small[pl.ds(4, 1), :]).astype(bf16)

    loop(count // BLOCK, first_norm)
    pump(7)

    def up(u):
        ready(4 + u)
        bias = jnp.concatenate(
            [
                small[pl.ds(8 + c * 2 + u // 2, 1), pl.ds((u % 2) * HALF, HALF)]
                for c in range(2)
            ],
            axis=1,
        )

        def block(r):
            rows = tile(r, ROWS)
            for j in range(3):
                cols = pl.ds(j * QUAD, QUAD)
                upper = nn(first[rows, :], unit_cols(4 + u, cols)) + bias[:, j * QUAD : (j + 1) * QUAD]
                share = 0.5 + 0.5 * lax.erf(upper * 0.7071067811865476)
                hidden[u, rows, cols] = (upper * share).astype(bf16)
                slope[u, rows, cols] = (
                    share + upper * (0.3989422804014327 * jnp.exp(-0.5 * upper * upper))
                ).astype(bf16)

        loop(count // ROWS, block)

    def down(u):
        ready(8 + u)

        def block(r):
            rows = tile(r, ROWS)
            term = nt(hidden[u, rows, :], weights(8 + u))
            back[rows, :] = term if u == 0 else back[rows, :] + term

        loop(count // ROWS, block)

    up(0)
    up(1)
    pump(8)
    up(2)
    pump(9)
    up(3)
    down(0)
    pump(10)
    down(1)
    pump(11)
    down(2)
    down(3)
    if comm:
        for u in range(UNITS):
            ag_sent(u)
    cot_copy.wait()

    def flip(source, target):
        for j in range(WIDE // LANES):
            cols = pl.ds(j * LANES, LANES)
            target[cols, :] = source[:, cols].T

    def second_norm(r):
        rows = tile(r, BLOCK)
        value = (
            normed[rows, :] * small[pl.ds(3, 1), :]
            + small[pl.ds(4, 1), :]
            + back[rows, :]
            + small[pl.ds(5, 1), :]
        )
        center = value - mean_last(value)
        root = lax.rsqrt(mean_last(center * center) + NORM_EPS)
        scaled = center * root
        upstream = cot[rows, :].astype(f32)
        cot[rows, :] = (scaled * small[pl.ds(6, 1), :] + small[pl.ds(7, 1), :]).astype(bf16)
        gained = upstream * small[pl.ds(6, 1), :]
        grad = (gained - mean_last(gained) - scaled * mean_last(gained * scaled)) * root
        back[rows, :] = grad
        low = grad.astype(bf16)
        own[rows, :] = low
        sums[5] += fold_rows(low.astype(f32))
        sums[6] += fold_rows(upstream * scaled)
        sums[7] += fold_rows(upstream)

    loop(count // BLOCK, second_norm)
    out_copy.start()
    flip(own, flip_a)
    flip(first, flip_b)

    def outer(u, flipped, source):
        def block(r):
            part = nn(flipped[tile(r, WIDE // planes), :], source[...]).astype(bf16)
            unit[u, r] = part.reshape(unit.shape[2:])

        loop(planes, block)

    for u in range(4):

        def block(r, u=u):
            rows = tile(r, ROWS)
            for j in range(3):
                cols = pl.ds(j * QUAD, QUAD)
                low = (nn(own[rows, :], unit_cols(8 + u, cols)) * slope[u, rows, cols].astype(f32)).astype(
                    bf16
                )
                slope[u, rows, cols] = low
                up_sums[u, :, cols] += fold_rows(low.astype(f32))

        loop(count // ROWS, block)
        outer(8 + u, flip_a, hidden.at[u])
        if comm:
            rs_start(8 + u)

        def gather_first(r, u=u):
            rows = tile(r, ROWS)
            back[rows, :] += nt(slope[u, rows, :], weights(4 + u))

        loop(count // ROWS, gather_first)
        outer(4 + u, flip_b, slope.at[u])
        if comm:
            rs_start(4 + u)
            rs_own(8 + u)
            if u >= 1:
                rs_own(4 + u - 1)
                rs_diag(8 + u - 1)
            if u >= 2:
                rs_diag(4 + u - 2)
                rs_line(8 + u - 2)

    def first_back(r):
        rows = tile(r, BLOCK)
        upstream = back[rows, :]
        scaled = normed[rows, :]
        gained = upstream * small[pl.ds(3, 1), :]
        grad = (gained - mean_last(gained) - scaled * mean_last(gained * scaled)) * inverse[rows, :]
        back[rows, :] = grad
        low = grad.astype(bf16)
        own[rows, :] = low
        sums[2] += fold_rows(low.astype(f32))
        sums[3] += fold_rows(upstream * scaled)
        sums[4] += fold_rows(upstream)

    loop(count // BLOCK, first_back)
    if comm:
        rs_own(7)
        rs_diag(11)
        rs_diag(6)
        rs_line(10)
        rs_line(4)
        rs_done(8)
    out_copy.wait()
    flip(own, flip_a)

    def mid_back(r):
        rows = tile(r, ROWS)
        for j in range(3):
            cols = pl.ds(j * QUAD, QUAD)
            cot[rows, cols] = nn(own[rows, :], unit_cols(3, cols)).astype(bf16)

    loop(count // ROWS, mid_back)
    for t in (chains * 3 - 2, chains * 3 - 1):
        probs_out(t).wait()
    probs_back(0).start()
    outer(3, flip_a, context)
    if comm:
        rs_start(3)
    own_again = pltpu.make_async_copy(tokens_hbm, own, local_sem.at[0])
    own_again.start()
    if comm:
        rs_diag(7)
        rs_line(11)
        rs_line(5)
        rs_done(9)
    own_again.wait()
    flip(own, flip_b)
    if comm:
        rs_own(3)

    for g in range(3):
        grads = hidden.at[g]

        def attend_back(chain):
            t = g * chains + chain
            probs_back(t).wait()

            @pl.when(t + 1 < 3 * chains)
            def _():
                probs_back(t + 1).start()

            rows = tile(chain, length)
            here = packed.at[g]
            queries = spread_heads(pair(here, rows, 0))
            keys = pair(here, rows, LANES)
            values = pair(here, rows, 2 * LANES)
            d_context = spread_heads(pair(cot, rows, g * LANES))
            low = probs[t % 2]
            wide = low.astype(f32)
            d_probs = nt(d_context, values)
            inner = jnp.sum(wide * d_probs, axis=1, keepdims=True)
            d_scores = (wide * (d_probs - inner)).astype(bf16)
            d_queries = (pick_heads(nn(d_scores, keys), length) * HEAD ** (-0.5)).astype(bf16)
            d_keys = tn(d_scores, queries).astype(bf16)
            d_values = tn(low, d_context).astype(bf16)
            put_pair(grads, rows, 0, d_queries)
            put_pair(grads, rows, LANES, d_keys)
            put_pair(grads, rows, 2 * LANES, d_values)
            for row, piece in ((0, d_queries), (1, d_values)):
                folded = fold_rows(piece.astype(f32))
                for c in range(2):
                    cols = pl.ds(c * HALF + g * LANES, LANES)
                    sums[row, :, cols] += folded[:, c * LANES : (c + 1) * LANES]

        def back_first(chain):
            attend_back(chain)

        def back_second(chain):
            attend_back(chain + chains // 2)

        loop(chains // 2, back_first)
        if comm:
            if g == 0:
                rs_line(6)
                rs_done(10)
                rs_done(4)
            if g == 1:
                rs_own(0)
                rs_diag(3)
                rs_done(11)
                rs_done(5)
            if g == 2:
                rs_own(1)
                rs_diag(0)
                rs_line(3)
                rs_done(7)
        loop(chains - chains // 2, back_second)

        def tokens_back(r):
            rows = tile(r, ROWS)
            back[rows, :] += nt(grads[rows, :], weights(g))

        loop(count // ROWS, tokens_back)
        outer(g, flip_b, grads)
        if comm:
            rs_start(g)
            if g == 0:
                rs_line(7)
                rs_done(6)

    if comm:
        rs_own(2)
        rs_diag(1)
        rs_line(0)
        rs_done(3)
        rs_diag(2)
        rs_line(1)
        rs_done(0)
        rs_line(2)
        rs_done(1)
        rs_done(2)
        for u in range(UNITS):
            rs_sent(u)
    else:
        whole_out = pltpu.make_async_copy(unit, shard, local_sem.at[3])
        whole_out.start()
        whole_out.wait()

    vectors[pl.ds(0, 8), :] = jnp.sum(sums[...], axis=1)
    folded = jnp.sum(up_sums[...], axis=1)
    for u in range(4):
        for c in range(2):
            vectors[pl.ds(8 + c * 2 + u // 2, 1), pl.ds((u % 2) * HALF, HALF)] = folded[
                u : u + 1, c * HALF : (c + 1) * HALF
            ]


def run_layer(tokens, lengths, cotangent, attn_in, attn_out, ffn_in, ffn_out, small, ranks):
    rows_here = attn_in.shape[0]
    width = small.shape[1]
    flat = tokens.reshape(-1, width)
    count = flat.shape[0]
    chains = lengths.size
    length = tokens.shape[2]
    comm = ranks % 4 == 0 and rows_here % 16 == 0
    planes = ranks // 4 if comm else 4
    steps = planes - 1
    unit_shape = (UNITS, planes, 2, 2, width // (planes * 4), WIDE)
    vmem = pl.BlockSpec(memory_space=pltpu.VMEM)
    hbm = pl.BlockSpec(memory_space=pl.ANY)
    operands = [lengths, flat, cotangent.reshape(-1, width), small, attn_in, attn_out, ffn_in, ffn_out]
    in_specs = [pl.BlockSpec(memory_space=pltpu.SMEM), hbm, hbm] + [vmem] * 5
    if not comm:
        shard = own_shard(attn_in, attn_out, ffn_in, ffn_out)
        whole = lax.all_gather(shard, "dp", axis=1, tiled=True)
        whole = lax.all_gather(whole, "mp", axis=2, tiled=True)
        operands.append(whole.reshape(unit_shape))
        in_specs.append(hbm)
    shard_shape = (UNITS, rows_here, HALF)
    out_shape = (
        jax.ShapeDtypeStruct((count, width), bf16),
        jax.ShapeDtypeStruct((count, width), f32),
        jax.ShapeDtypeStruct(shard_shape, f32) if comm else jax.ShapeDtypeStruct(unit_shape, bf16),
        jax.ShapeDtypeStruct(small.shape, f32),
        jax.ShapeDtypeStruct((3 * chains, 4 * length, length), bf16),
    )
    out_specs = (hbm, vmem, vmem if comm else hbm, vmem, hbm)
    scratch = [
        pltpu.VMEM(unit_shape, bf16),
        pltpu.VMEM((3, count, WIDE), bf16),
        pltpu.VMEM((count, width), bf16),
        pltpu.VMEM((count, width), f32),
        pltpu.VMEM((count, 1), f32),
        pltpu.VMEM((count, width), bf16),
        pltpu.VMEM((4, count, WIDE), bf16),
        pltpu.VMEM((4, count, WIDE), bf16),
        pltpu.VMEM((count, width), bf16),
        pltpu.VMEM((count, width), bf16),
        pltpu.VMEM((width, count), bf16),
        pltpu.VMEM((width, count), bf16),
        pltpu.VMEM((2, 4 * length, length), bf16),
        pltpu.VMEM((8, 8, width), f32),
        pltpu.VMEM((4, 8, WIDE), f32),
        pltpu.SemaphoreType.DMA((4,)),
        pltpu.SemaphoreType.DMA((2,)),
    ]
    params = dict(vmem_limit_bytes=64 * 2**20 - 2**16)
    if comm:
        scratch += [
            pltpu.VMEM((UNITS, planes, 2, 2, rows_here, HALF), bf16),
            pltpu.VMEM((UNITS, planes, rows_here, HALF), bf16),
            pltpu.VMEM((UNITS, 2, planes, rows_here, HALF), bf16),
            pltpu.VMEM((UNITS, steps, rows_here, HALF), bf16),
            pltpu.SemaphoreType.DMA((UNITS, steps + 4)),
            pltpu.SemaphoreType.DMA((UNITS, steps + 4)),
            pltpu.SemaphoreType.DMA((UNITS, steps + 4)),
            pltpu.SemaphoreType.DMA((UNITS, steps + 4)),
        ]
        params.update(collective_id=0, has_side_effects=True)
    out, back, shard, vectors, _ = pl.pallas_call(
        functools.partial(main_kernel, comm),
        out_shape=out_shape,
        in_specs=in_specs,
        out_specs=out_specs,
        scratch_shapes=scratch,
        compiler_params=pltpu.CompilerParams(**params),
    )(*operands)
    if not comm:
        summed = shard.reshape(UNITS, width, 2, HALF).astype(f32)
        summed = lax.psum_scatter(summed, "mp", scatter_dimension=2, tiled=True)
        summed = lax.psum_scatter(
            summed.reshape(UNITS, width, HALF), "dp", scatter_dimension=1, tiled=True
        )
        shard = summed
    return out.reshape(tokens.shape), back.reshape(tokens.shape), shard, vectors


def own_shard(attn_in, attn_out, ffn_in, ffn_out):
    rows = attn_in.shape[0]
    heads = [
        attn_in[:, :, g * LANES : (g + 1) * LANES].reshape(rows, HALF) for g in range(3)
    ]
    up = [ffn_in[:, u * HALF : (u + 1) * HALF] for u in range(4)]
    down = [ffn_out[u * HALF : (u + 1) * HALF].T for u in range(4)]
    return jnp.stack(heads + [attn_out.T] + up + down).astype(bf16)


def adam_moments(gradient, first_moment, second_moment):
    first_new = BETA_FIRST * first_moment + (1.0 - BETA_FIRST) * gradient
    second_new = BETA_SECOND * second_moment + (1.0 - BETA_SECOND) * gradient * gradient
    direction = (
        first_new
        / (1.0 - BETA_FIRST**STEP)
        / (jnp.sqrt(second_new / (1.0 - BETA_SECOND**STEP)) + ADAM_EPS)
    )
    return (first_new, second_new, direction)


def body(
    ranks,
    tokens,
    lengths,
    cotangent,
    attn_in,
    attn_out,
    ffn_in,
    ffn_out,
    attn_in_first,
    attn_in_second,
    attn_out_first,
    attn_out_second,
    ffn_in_first,
    ffn_in_second,
    ffn_out_first,
    ffn_out_second,
    small,
    small_first,
    small_second,
):
    output, tokens_grad, shard, vectors = run_layer(
        tokens, lengths, cotangent, attn_in, attn_out, ffn_in, ffn_out, small, ranks
    )
    rows = attn_in.shape[0]
    grad_in = jnp.concatenate([shard[g].reshape(rows, 3, LANES) for g in range(3)], axis=2)
    grad_mid = shard[3].T
    grad_up = jnp.concatenate([shard[4 + u] for u in range(4)], axis=1)
    grad_down = jnp.concatenate([shard[8 + u].T for u in range(4)], axis=0)
    matrices = (
        (attn_in, grad_in, attn_in_first, attn_in_second),
        (attn_out, grad_mid, attn_out_first, attn_out_second),
        (ffn_in, grad_up, ffn_in_first, ffn_in_second),
        (ffn_out, grad_down, ffn_out_first, ffn_out_second),
    )
    moments = [adam_moments(entry[1], entry[2], entry[3]) for entry in matrices]
    headings = [moments[i][2] + DECAY_RATE * matrices[i][0] for i in range(4)]
    weight_squares = jnp.stack([jnp.sum(entry[0] * entry[0]) for entry in matrices])
    step_squares = jnp.stack([jnp.sum(heading * heading) for heading in headings])
    vector_grad, weight_sums, step_sums = lax.psum(
        (vectors, weight_squares, step_squares), ("dp", "mp")
    )
    weight_norms = jnp.sqrt(weight_sums)
    step_norms = jnp.sqrt(step_sums)
    results = [output, tokens_grad]
    for i in range(4):
        weight = matrices[i][0]
        renewed = weight - RATE_MATRIX * (weight_norms[i] / step_norms[i]) * headings[i]
        results.extend(
            [matrices[i][1], moments[i][0], moments[i][1], renewed, renewed.astype(bf16)]
        )
    small_first_new, small_second_new, small_direction = adam_moments(
        vector_grad, small_first, small_second
    )
    small_new = small - RATE_VECTOR * small_direction
    results.extend(
        [
            vector_grad,
            small_first_new,
            small_second_new,
            small_new,
            jnp.stack((weight_norms, step_norms)),
        ]
    )
    return tuple(results)


def solution(mesh):
    chains = P(None, ("dp", "mp"), None, None)
    rows_three = P("dp", None, "mp")
    rows_two = P("dp", "mp")
    columns = P("mp", "dp")
    whole = P()
    return jax.shard_map(
        functools.partial(body, mesh.shape["dp"]),
        mesh=mesh,
        in_specs=(
            chains,
            P(None, ("dp", "mp")),
            chains,
            rows_three,
            columns,
            rows_two,
            columns,
            rows_three,
            rows_three,
            columns,
            columns,
            rows_two,
            rows_two,
            columns,
            columns,
            whole,
            whole,
            whole,
        ),
        out_specs=(
            (chains, chains)
            + (rows_three,) * 5
            + (columns,) * 5
            + (rows_two,) * 5
            + (columns,) * 5
            + (whole,) * 5
        ),
        check_vma=False,
    )
```

time: 1130 us -> 278 us (0.25); the launches traced: 1120 us -> 277 us
  waiting for transfers between devices: 569 us -> 0 us
  Pallas kernels: 0 us -> 203 us
  matrix products: 184 us -> 0 us
  local copies, waits for them, and re-layouts: 171 us -> 12.3 us
  other arithmetic: 76.1 us -> 16.1 us
  blocking collectives: 92.6 us -> 39.8 us
  between operations: 21.8 us -> 6.33 us
    reduce_scatter x12 -> x0, waiting for transfers between devices: 417 us -> none  [the longest x1 136 us: reduce_weights(): lax.psum_scatter(local_grads[0], 'dp', scatter_dimension=0, tiled=True)]
    pallas_call x0 -> x1, Pallas kernels: none -> 203 us  [run_layer(): pl.pallas_call(functools.partial(main_kernel, comm), out_shape=out_shape,...]
    dot_general x36 -> x0, matrix products: 184 us -> none  [the longest x8 50.1 us: times_transposed(): lax.dot_general(left, right, (((1,), (1,)), ((), ())), preferred_element_...]
    all_gather x11 -> x0, waiting for transfers between devices: 149 us -> none  [the longest x1 60 us: body(): lax.all_gather(ffn_in.astype(jnp.bfloat16), 'dp', axis=0, tiled=True)]
    all_gather x1 -> x0, blocking collectives: 49.4 us -> none  [body(): lax.all_gather(attn_out.astype(jnp.bfloat16), 'dp', axis=1, tiled=True)]
    another operation x32 -> x3, local copies, waits for them, and re-layouts: 47.6 us -> 0.09 us  [body(): shard[g].reshape(rows, 3, LANES)]
    reduce_sum x14 -> x0, other arithmetic: 26.4 us -> none  [the longest x3 12 us: norm_back(): jnp.sum(upstream * normed, axis=(0, 1))]
    convert_element_type x12 -> x0, local copies, waits for them, and re-layouts: 23.8 us -> none  [the longest x4 7.69 us: body(): key_rows = packed[:, 1].astype(jnp.bfloat16).reshape(head_shape)]
  transfers between devices with their start and end apart: 23 -> 0, of which waited for: 19 -> 0; matrix products, arithmetic and copies ran while one was open for 28% -> 0% of each run, Pallas kernels for 0% -> 0%
where the time goes in v1:
time: 278 us; the launch traced here: 277 us
  Pallas kernels  203 us (73%)
  blocking collectives  39.8 us (14%)
  other arithmetic  16.1 us (6%)
  local copies, waits for them, and re-layouts  12.3 us (4%)
  between operations  6.33 us (2%)
    pallas_call x1, Pallas kernels, run_layer(): pl.pallas_call(functools.partial(main_kernel, comm), out_shape=out_shape,...  203 us
    psum x1, blocking collectives, body(): lax.psum((vectors, weight_squares, step_squares), ('dp', 'mp'))  39.8 us
    unnamed x59, local copies, waits for them, and re-layouts  9.72 us
    reduce_sum x4, other arithmetic, body(): jnp.sum(heading * heading)  6.14 us

profile of v1, /device:TPU:0, one launch (start us, length us, event | category | flops | bytes accessed | tf_op | source)
XLA Modules:
  0.0 277.1 jit_solution(816656063205507602)
XLA Ops:
  0.7 1.7 copy.64.w_mid
  2.4 1.8 copy.63.w_in
  4.1 2.1 copy.65.w_down
  6.2 202.5 %shard_map.385 = (bf16[960,768]{1,0:T(8,128)(2,1)}, f32[960,768]{1,0:T(8,128)}, f32[12,48,384]{2,1,0:T(8,128)}, f32[12,768]{1,0:T(8,128)}, bf16[18,640,160]{2,1,0:T(8,128)(2,1)}) custom-call(s32[2,3]{1,0:T(2,128)} %lengths.1, bf16[960,768]{1,0:T(8,128)(2,1)} %bitcast.50, bf16[960,768]{1,0:T(8,128)(2,1)} %bitcast.51, f32[12,768]{1,0:T(8,128)} %small.1, ...), custom_call_target="tpu_custom_call" | custom-call | tf_op jit(solution)/shard_map/pallas_call | solution.py:797
  208.8 0.0 copy-start.3
  208.8 0.0 copy-start.19
  208.8 0.0 copy-start.20
  208.8 2.3 multiply_reduce_fusion.6
  211.1 1.3 slice_bitcast_fusion.7
  212.4 0.0 copy-start.1
  212.5 0.0 copy-start.13
  212.5 0.0 copy-start.14
  212.6 0.0 copy-done.3
  212.7 0.0 copy-done.19
  212.7 0.0 copy-done.20
  212.7 0.0 copy-start.12
  212.7 0.0 copy-start.2
  212.7 0.0 copy-start.15
  212.7 0.0 copy-start.16
  212.7 0.9 multiply_reduce_fusion.4
  213.6 0.0 copy-done.1
  213.6 0.0 copy-done.14
  213.6 1.5 multiply_reduce_fusion.1
  215.1 0.0 copy-start.11
  215.1 0.0 copy-start.21
  215.2 0.0 copy-start.23
  215.2 0.0 copy-start.24
  215.2 1.5 multiply_reduce_fusion
  216.7 2.7 pad_maximum_fusion.4
  219.4 2.7 pad_maximum_fusion.3
  222.0 39.8 %all-reduce = (f32[4]{0:T(128)S(1)}, f32[4]{0:T(128)S(1)}, f32[12,768]{1,0:T(8,128)S(1)}) all-reduce(f32[4]{0:T(128)S(1)} %pad_maximum_fusion.3, f32[4]{0:T(128)S(1)} %pad_maximum_fusion.4, f32[12,768]{1,0:T(8,128)S(1)} %copy-done.22), channel_id=1, replica_groups=mesh['dp'=16,'mp'=2] {'dp','mp'}, use_global_device_ids=true, to_apply=%region_4.0 | all-reduce | flops 9224 | bytes 73792 | tf_op jit(solution)/shard_map/psum | solution.py:875
  261.9 0.0 copy-start.25
  261.9 0.6 pad_maximum_fusion.2
  262.5 0.6 fusion.14
  263.0 0.6 fusion.15
  269.0 0.0 copy-done.17
  269.0 0.0 copy-done.18
  269.0 0.0 copy-done.11
  269.0 0.7 fusion.8
  269.7 0.0 copy-done.24
  269.7 0.7 multiply_subtract_fusion.4
  270.4 0.0 copy-done.10
  270.4 0.9 fusion.9
  271.3 0.9 fusion.6
  272.2 0.9 fusion.7
  273.1 1.1 copy.76
  274.3 1.3 copy-done
  275.5 1.6 copy.77
  (33 shorter events, 0.2 us)
Async XLA Ops:
  208.8 3.9 %copy-start.3 = (f32[48,3,384]{2,0,1:T(8,128)S(1)}, f32[48,3,384]{2,0,1:T(8,128)}, u32[]{:S(2)}) copy-start(f32[48,3,384]{2,0,1:T(8,128)} %param.21) | copy-start | bytes 663556
  208.8 3.9 %copy-start.19 = (f32[48,3,384]{2,0,1:T(8,128)S(1)}, f32[48,3,384]{2,0,1:T(8,128)}, u32[]{:S(2)}) copy-start(f32[48,3,384]{2,0,1:T(8,128)} %param.26) | copy-start | bytes 663556
  208.8 3.9 %copy-start.20 = (f32[48,3,384]{2,0,1:T(8,128)S(1)}, f32[48,3,384]{2,0,1:T(8,128)}, u32[]{:S(2)}) copy-start(f32[48,3,384]{2,0,1:T(8,128)} %param.25) | copy-start | bytes 663556
  211.1 57.9 %copy-start.17 = (f32[384,48]{0,1:T(8,128)}, f32[384,48]{0,1:T(8,128)S(1)}, u32[]{:S(2)}) copy-start(f32[384,48]{0,1:T(8,128)S(1)} %get-tuple-element.155) | copy-start | bytes 221188
  211.1 57.9 %copy-start.18 = (f32[384,48]{0,1:T(8,128)}, f32[384,48]{0,1:T(8,128)S(1)}, u32[]{:S(2)}) copy-start(f32[384,48]{0,1:T(8,128)S(1)} %get-tuple-element.156) | copy-start | bytes 221188
  212.4 1.1 copy-start.1
  212.5 1.1 copy-start.13
  212.5 1.2 copy-start.14
  212.7 2.4 copy-start.12
  212.7 2.5 copy-start.2
  212.7 2.5 copy-start.15
  212.7 2.5 copy-start.16
  213.6 56.8 %copy-start.9 = (f32[48,3,384]{2,0,1:T(8,128)}, f32[48,3,384]{2,0,1:T(8,128)S(1)}, u32[]{:S(2)}) copy-start(f32[48,3,384]{2,0,1:T(8,128)S(1)} %get-tuple-element.151) | copy-start | bytes 663556
  213.6 56.8 %copy-start.10 = (f32[48,3,384]{2,0,1:T(8,128)}, f32[48,3,384]{2,0,1:T(8,128)S(1)}, u32[]{:S(2)}) copy-start(f32[48,3,384]{2,0,1:T(8,128)S(1)} %get-tuple-element.150) | copy-start | bytes 663556
  215.1 57.1 %copy-start.5 = (f32[48,1536]{1,0:T(8,128)}, f32[48,1536]{1,0:T(8,128)S(1)}, u32[]{:S(2)}) copy-start(f32[48,1536]{1,0:T(8,128)S(1)} %get-tuple-element.160) | copy-start | bytes 884740
  215.1 57.1 %copy-start.6 = (f32[48,1536]{1,0:T(8,128)}, f32[48,1536]{1,0:T(8,128)S(1)}, u32[]{:S(2)}) copy-start(f32[48,1536]{1,0:T(8,128)S(1)} %get-tuple-element.161) | copy-start | bytes 884740
  215.1 6.9 %copy-start.22 = (f32[12,768]{1,0:T(8,128)S(1)}, f32[12,768]{1,0:T(8,128)}, u32[]{:S(2)}) copy-start(f32[12,768]{1,0:T(8,128)} %get-tuple-element.34) | copy-start | bytes 110596
  215.1 53.9 %copy-start.11 = (f32[384,48]{0,1:T(8,128)S(1)}, f32[384,48]{0,1:T(8,128)}, u32[]{:S(2)}) copy-start(f32[384,48]{0,1:T(8,128)} %param.22) | copy-start | bytes 221188
  215.1 54.6 %copy-start.21 = (f32[12,768]{1,0:T(8,128)S(1)}, f32[12,768]{1,0:T(8,128)}, u32[]{:S(2)}) copy-start(f32[12,768]{1,0:T(8,128)} %small.1) | copy-start | bytes 110596
  215.2 54.6 %copy-start.23 = (f32[12,768]{1,0:T(8,128)S(1)}, f32[12,768]{1,0:T(8,128)}, u32[]{:S(2)}) copy-start(f32[12,768]{1,0:T(8,128)} %param.35) | copy-start | bytes 110596
  215.2 54.6 %copy-start.24 = (f32[12,768]{1,0:T(8,128)S(1)}, f32[12,768]{1,0:T(8,128)}, u32[]{:S(2)}) copy-start(f32[12,768]{1,0:T(8,128)} %param.34) | copy-start | bytes 110596
  216.7 55.5 %copy-start.7 = (f32[1536,48]{0,1:T(8,128)}, f32[1536,48]{0,1:T(8,128)S(1)}, u32[]{:S(2)}) copy-start(f32[1536,48]{0,1:T(8,128)S(1)} %get-tuple-element.165) | copy-start | bytes 884740
  216.7 55.5 %copy-start.8 = (f32[1536,48]{0,1:T(8,128)}, f32[1536,48]{0,1:T(8,128)S(1)}, u32[]{:S(2)}) copy-start(f32[1536,48]{0,1:T(8,128)S(1)} %get-tuple-element.166) | copy-start | bytes 884740
  261.9 10.3 %copy-start.25 = (f32[12,768]{1,0:T(8,128)}, f32[12,768]{1,0:T(8,128)S(1)}, u32[]{:S(2)}) copy-start(f32[12,768]{1,0:T(8,128)S(1)} %get-tuple-element.169) | copy-start | bytes 110596
  271.3 1.9 copy-start.4
  273.1 2.4 copy-start
